TPU v7x, 32 devices: a whole 2x2x4 slice. The times are simulated.
32 devices in a mesh: seq: 4 (over y, x), fsdp: 8 (over z, core).
Axes of the slice: x: 2, y: 2, z: 4, core: 2. Of those that a mesh axis runs over, the one named last changes fastest.
Arguments:
- inputs: bfloat16 [8, 1024, 1536], P('fsdp', 'seq'), may hold values from -6 to 6
- cotangent: bfloat16 [8, 1024, 1536], P('fsdp', 'seq'), may hold values from -6 to 6
- qkv_weight: float32 [1536, 3072], P('fsdp'), may hold values from -0.15625 to 0.15625
- out_weight: float32 [1536, 1536], P('fsdp'), may hold values from -1.75 to 1.75
- gate_up_weight: float32 [1536, 8192], P('fsdp'), may hold values from -0.15625 to 0.15625
- down_weight: float32 [4096, 1536], P('fsdp'), may hold values from -0.09375 to 0.09375
- norm_gains: float32 [2, 1536], P(None, 'fsdp'), may hold values from 0.5 to 1.5
- qkv_first: float32 [1536, 3072], P('fsdp'), may hold values from -40 to 40
- qkv_second: float32 [1536, 3072], P('fsdp'), may hold values from 212.992 to 860.16
- out_first: float32 [1536, 1536], P('fsdp'), may hold values from -3.5 to 3.5
- out_second: float32 [1536, 1536], P('fsdp'), may hold values from 1.55648 to 6.22592
- gate_up_first: float32 [1536, 8192], P('fsdp'), may hold values from -24 to 24
- gate_up_second: float32 [1536, 8192], P('fsdp'), may hold values from 68.8128 to 278.528
- down_first: float32 [4096, 1536], P('fsdp'), may hold values from -32 to 32
- down_second: float32 [4096, 1536], P('fsdp'), may hold values from 155.648 to 622.592
- gain_first: float32 [2, 1536], P(None, 'fsdp'), may hold values from -64 to 64
- gain_second: float32 [2, 1536], P(None, 'fsdp'), may hold values from 434.176 to 1720.32
Outputs:
- block_out: bfloat16 [8, 1024, 1536], P('fsdp', 'seq')
- input_grad: float32 [8, 1024, 1536], P('fsdp', 'seq')
- qkv_weight_new: float32 [1536, 3072], P('fsdp')
- qkv_first_new: float32 [1536, 3072], P('fsdp')
- qkv_second_new: float32 [1536, 3072], P('fsdp')
- out_weight_new: float32 [1536, 1536], P('fsdp')
- out_first_new: float32 [1536, 1536], P('fsdp')
- out_second_new: float32 [1536, 1536], P('fsdp')
- gate_up_weight_new: float32 [1536, 8192], P('fsdp')
- gate_up_first_new: float32 [1536, 8192], P('fsdp')
- gate_up_second_new: float32 [1536, 8192], P('fsdp')
- down_weight_new: float32 [4096, 1536], P('fsdp')
- down_first_new: float32 [4096, 1536], P('fsdp')
- down_second_new: float32 [4096, 1536], P('fsdp')
- norm_gains_new: float32 [2, 1536], P(None, 'fsdp')
- gain_first_new: float32 [2, 1536], P(None, 'fsdp')
- gain_second_new: float32 [2, 1536], P(None, 'fsdp')
All inputs are finite; a program needn't handle non-finite values.
Results may differ from a plain program's by a relative error of at most 0.03.
Values may be sent and summed in bfloat16 or wider, within the bound.
A program may use at most 384 MiB of HBM per device.

v0:
```python
import functools

import jax
import jax.numpy as jnp
import ml_dtypes
import numpy as np
from jax import lax
from jax.experimental import pallas as pl
from jax.experimental.pallas import tpu as pltpu
from jax.sharding import PartitionSpec as P

HEAD_DIM = 96
KV_HEADS = 8
ADAM_STEP = 10
GROUP = 2

NORM_EPS = 1e-05
ROPE_BASE = 100000.0
BETA_ONE = 0.9
BETA_TWO = 0.95
ADAM_EPS = 1e-08
WEIGHT_DECAY = 0.1
RATE_QKV = 0.07
RATE_OUT = 0.8
RATE_GATE_UP = 0.07
RATE_DOWN = 0.045
RATE_GAINS = 0.6
BF = jnp.bfloat16
F32 = jnp.float32
VMEM_LIMIT = 62 * 1024 * 1024
BACK_LIMIT = 42 * 1024 * 1024


MESH = pl.DeviceIdType.MESH


def rdma(src, dst, ssem, rsem, dev):
    return pltpu.make_async_remote_copy(
        src_ref=src, dst_ref=dst, send_sem=ssem, recv_sem=rsem, device_id=dev, device_id_type=MESH
    )


class Place:
    def __init__(self, n, sib, planes):
        self.n, self.sib, self.planes = n, sib, planes
        self.s = lax.axis_index("seq")
        self.f = lax.axis_index("fsdp")
        self.c = lax.rem(self.f, sib)
        self.p = lax.div(self.f, sib)
        a, b = lax.div(self.s, 2), lax.rem(self.s, 2)
        self.r = a * (1 - b) + (n - 1 - a) * b

    def seq_at(self, j):
        if j == 0:
            return self.s
        n = self.n
        q = lax.rem(self.r + (j + n), n)
        t = lax.div(q, n // 2)
        return (1 - t) * 2 * q + t * (2 * (n - 1 - q) + 1)

    def dev(self, s, c):
        return (s, self.p * self.sib + c)

    def col(self, dp, dc):
        return lax.rem(self.p + dp, self.planes) * self.sib + lax.rem(self.c + dc, self.sib)

    def barrier(self):
        sem = pltpu.get_barrier_semaphore()
        group = self.n * self.sib
        tau = self.s * self.sib + self.c
        for j in range(1, group):
            t = lax.rem(tau + j, group)
            pl.semaphore_signal(
                sem, inc=1, device_id=self.dev(lax.div(t, self.sib), lax.rem(t, self.sib)),
                device_id_type=MESH,
            )
        for dp in range(1, self.planes):
            for dc in range(self.sib):
                pl.semaphore_signal(
                    sem, inc=1, device_id=(self.s, self.col(dp, dc)), device_id_type=MESH
                )
        pl.semaphore_wait(sem, group - 1 + (self.planes - 1) * self.sib)


class Gather:
    def __init__(self, at, part, sems):
        self.at, self.part = at, part
        self.ring_s, self.ring_r = sems[:2]
        self.share = at.sib > 1 and len(sems) > 2
        if self.share:
            self.sib_s, self.sib_r = sems[2:]
        self.sent = []

    @staticmethod
    def scratch(n, share=True):
        d = pltpu.SemaphoreType.DMA
        ring = [d((2, n // 2, 2)), d((2, n // 2, 2))]
        return ring + [d((n, 2)), d((n, 2))] if share else ring

    def _send(self, copy):
        copy.start()
        self.sent.append(copy)

    def _ring(self, way, hop, half):
        at = self.at
        src = self.part(at.c, at.seq_at(-(hop - 1) if way == 0 else hop - 1), half)
        to = at.dev(at.seq_at(1 if way == 0 else -1), at.c)
        self._send(
            rdma(src, src, self.ring_s.at[way, hop - 1, half], self.ring_r.at[way, hop - 1, half], to)
        )

    def _sib(self, j, half):
        at = self.at
        if self.share:
            src = self.part(at.c, at.seq_at(j), half)
            slot = j % at.n
            self._send(
                rdma(src, src, self.sib_s.at[slot, half], self.sib_r.at[slot, half],
                     at.dev(at.s, 1 - at.c))
            )

    def start(self):
        self._ring(0, 1, 0)
        self._ring(1, 1, 1)
        self._ring(0, 1, 1)
        self._ring(1, 1, 0)
        self._sib(0, 0)
        self._sib(0, 1)

    def _arrive(self, way, hop, half):
        at = self.at
        j = -hop if way == 0 else hop
        ref = self.part(at.c, at.seq_at(j), half)
        rdma(ref, ref, self.ring_s.at[way, hop - 1, half], self.ring_r.at[way, hop - 1, half],
             at.dev(at.s, at.c)).wait_recv()
        last = at.n // 2
        if hop + 1 < last or (hop + 1 == last and half == way):
            self._ring(way, hop + 1, half)
        if hop == last:
            j = last
        self._sib(j, half)

    def hop(self, hop):
        self.hop_first(hop)
        self.hop_second(hop)

    def hop_first(self, hop):
        self._arrive(0, hop, 0)
        self._arrive(1, hop, 1)

    def hop_second(self, hop):
        if hop < self.at.n // 2:
            self._arrive(0, hop, 1)
            self._arrive(1, hop, 0)

    def sib_wait(self, j):
        at = self.at
        if self.share:
            for half in range(2):
                ref = self.part(1 - at.c, at.seq_at(j), half)
                slot = j % at.n
                rdma(ref, ref, self.sib_s.at[slot, half], self.sib_r.at[slot, half],
                     at.dev(at.s, at.c)).wait_recv()

    def stages(self):
        last = self.at.n // 2
        yield 0, [0]
        for h in range(1, last):
            yield h, [-h, h]
        yield last, [last]

    def wait_stage(self, h, offsets):
        if h:
            self.hop(h)
        for j in offsets:
            self.sib_wait(j)

    def drain(self):
        for copy in self.sent:
            copy.wait_send()


class Move:
    def __init__(self, at, src, dst, sems, every_core=True):
        self.at, self.src, self.dst = at, src, dst
        self.ssem, self.rsem, self.hop, self.own = sems
        self.cores = at.sib if every_core else 1
        self.relay = at.planes == 4

    @staticmethod
    def sems(planes, sib):
        d = pltpu.SemaphoreType.DMA
        return [d((planes, sib)), d((planes, sib)), d((sib,)), d((1,))]

    def _pairs(self):
        for dp in [2, 1, 3] if self.relay else range(1, self.at.planes):
            for dc in range(self.cores):
                yield dp, dc
        for dc in range(1, self.cores):
            yield 0, dc

    def _direct(self, dp, body):
        if self.relay and dp in (1, 3):
            pl.when(self.at.p != (3 if dp == 1 else 0))(body)
        else:
            body()

    def _send(self, dp, dc):
        at = self.at
        return rdma(self.src(lax.rem(at.c + dc, at.sib)), self.dst(at.f), self.ssem.at[dp, dc],
                    self.rsem.at[dp, dc], (at.s, at.col(dp, dc)))

    def _local(self):
        return pltpu.make_async_copy(self.src(self.at.c), self.dst(self.at.f), self.own.at[0])

    def start(self):
        self.start_far()
        self.start_near()

    def start_far(self):
        for dp, dc in self._pairs():
            if self.relay and dp == 2:
                self._send(dp, dc).start()

    def start_near(self):
        self._local().start()
        for dp, dc in self._pairs():
            if not (self.relay and dp == 2):
                self._direct(dp, lambda: self._send(dp, dc).start())

    def _got(self, dp, dc):
        at = self.at
        source = lax.rem(at.p - dp + at.planes, at.planes) * at.sib + lax.rem(
            at.c - dc + at.sib, at.sib
        )
        ref = self.dst(source)
        rdma(ref, ref, self.ssem.at[dp, dc], self.rsem.at[dp, dc], (at.s, at.f)).wait_recv()
        return ref

    def pass_on(self):
        at = self.at
        if not self.relay:
            return
        for dp, dc in self._pairs():
            if dp == 2:
                ref = self._got(dp, dc)
                for here, to, slot in ((2, 3, 3), (1, 0, 1)):
                    @pl.when(at.p == here)
                    def _():
                        rdma(ref, ref, self.hop.at[dc], self.rsem.at[slot, dc],
                             (at.s, to * at.sib + at.c)).start()

    def wait(self):
        for dp, dc in self._pairs():
            if not (self.relay and dp == 2):
                self._got(dp, dc)
        self._local().wait()

    def drain(self):
        at = self.at
        for dp, dc in self._pairs():
            self._direct(dp, lambda: self._send(dp, dc).wait_send())
            if self.relay and dp == 2:
                ref = self.dst(at.f)

                @pl.when(jnp.logical_or(at.p == 1, at.p == 2))
                def _():
                    rdma(ref, ref, self.hop.at[dc], self.rsem.at[0, dc], (at.s, at.f)).wait_send()


class Scatter:
    def __init__(self, at, bufs, sems, rows, cols):
        self.at, self.rows, self.cols = at, rows, pl.ds(0, cols)
        self.stage, self.sib_in, self.out, self.inn = bufs
        self.sib_s, self.sib_r, self.ring_s, self.ring_r = sems
        self.sent, self.handed = [], []

    @staticmethod
    def scratch(n, shape):
        return [
            pltpu.VMEM((2, *shape), BF), pltpu.VMEM((n, *shape), BF),
            pltpu.VMEM((2, n // 2, *shape), BF), pltpu.VMEM((2, n // 2, *shape), BF),
        ]

    @staticmethod
    def views(stage, sib_in, out, inn):
        return (
            lambda k: stage.at[k], lambda k: sib_in.at[k],
            lambda w, k: out.at[w, k], lambda w, k: inn.at[w, k],
        )

    @staticmethod
    def sems(n):
        d = pltpu.SemaphoreType.DMA
        return [d((n,)), d((n,)), d((2, n // 2)), d((2, n // 2))]

    def offsets(self):
        last = self.at.n // 2
        order = [last]
        for h in range(last - 1, 0, -1):
            order += [h, -h]
        return order + [0]

    def to_sibling(self, k, produce):
        at = self.at
        if at.sib == 1:
            return
        if k >= 2:
            self.handed[k - 2].wait_send()
        view = self.stage(k % 2).at[pl.ds(0, self.rows), self.cols]
        produce(1 - at.c, at.seq_at(self.offsets()[k]), view)
        copy = rdma(view, self.sib_in(k).at[pl.ds(0, self.rows), self.cols],
                    self.sib_s.at[k], self.sib_r.at[k], at.dev(at.s, 1 - at.c))
        copy.start()
        self.handed.append(copy)

    def open(self, stage, ring, finish):
        self.to_sibling(0, stage)
        self.step(0, ring, finish)
        for k in range(1, len(self.offsets())):
            self.to_sibling(k, stage)

    def _send(self, way, k, rows):
        at = self.at
        src = self.out(way, k).at[rows, self.cols]
        copy = rdma(src, self.inn(way, k).at[rows, self.cols], self.ring_s.at[way, k], self.ring_r.at[way, k],
                    at.dev(at.seq_at(1 if way == 0 else -1), at.c))
        copy.start()
        self.sent.append(copy)

    def _wait(self, way, k, rows):
        ref = self.inn(way, k).at[rows, self.cols]
        at = self.at
        rdma(ref, ref, self.ring_s.at[way, k], self.ring_r.at[way, k],
             at.dev(at.s, at.c)).wait_recv()

    def step(self, k, produce, finish):
        at = self.at
        last = at.n // 2
        length = self.rows
        half = length // 2
        halves = (pl.ds(0, half), pl.ds(half, half))
        whole = pl.ds(0, length)
        j = self.offsets()[k]
        if at.sib > 1:
            ref = self.sib_in(k).at[pl.ds(0, length), self.cols]
            rdma(ref, ref, self.sib_s.at[k], self.sib_r.at[k], at.dev(at.s, at.c)).wait_recv()
        h = abs(j)
        if h == last:
            got = []
        else:
            ways = (0, 1) if h == 0 else ((0,) if j > 0 else (1,))
            rows_in = [halves[w] if h + 1 == last else whole for w in ways]
            got = [(w, rw) for w, rw in zip(ways, rows_in)]
        pending = [True]

        def store(cols, value, k=k, h=h, j=j, got=got, pending=pending):
            if pending[0]:
                for w, rw in got:
                    self._wait(w, h, rw)
                pending[0] = False
            if at.sib > 1:
                value = value + self.sib_in(k)[pl.ds(0, length), cols].astype(F32)
            for w, rw in got:
                if h + 1 == last:
                    add = self.inn(w, h)[pl.ds(w * half, half), cols].astype(F32)
                    if w == 0:
                        value = jnp.concatenate([value[:half] + add, value[half:]], axis=0)
                    else:
                        value = jnp.concatenate([value[:half], value[half:] + add], axis=0)
                else:
                    value = value + self.inn(w, h)[pl.ds(0, length), cols].astype(F32)
            if h == last:
                low = value.astype(BF)
                self.out(0, h - 1)[pl.ds(0, half), cols] = low[:half]
                self.out(1, h - 1)[pl.ds(half, half), cols] = low[half:]
            elif h:
                self.out(0 if j > 0 else 1, h - 1)[pl.ds(0, length), cols] = value.astype(BF)
            else:
                finish(cols, value)

        produce(at.c, at.seq_at(j), store)
        if h == last:
            self._send(0, h - 1, halves[0])
            self._send(1, h - 1, halves[1])
        elif h:
            self._send(0 if j > 0 else 1, h - 1, whole)

    def drain(self):
        for copy in self.sent + self.handed[-2:]:
            copy.wait_send()


class Credits:
    def __init__(self, at, sem):
        self.at, self.sem = at, sem

    def give(self):
        at = self.at
        if at.sib > 1:
            pl.semaphore_signal(
                self.sem, inc=1, device_id=at.dev(at.s, 1 - at.c), device_id_type=MESH
            )
        for way in (1, -1):
            pl.semaphore_signal(
                self.sem, inc=1, device_id=at.dev(at.seq_at(way), at.c), device_id_type=MESH
            )

    def take(self):
        pl.semaphore_wait(self.sem, 3 if self.at.sib > 1 else 2)


def nt(a, b):
    return lax.dot_general(a, b, (((1,), (1,)), ((), ())), preferred_element_type=F32)


def tn(a, b):
    return lax.dot_general(a, b, (((0,), (0,)), ((), ())), preferred_element_type=F32)


def nn(a, b):
    return lax.dot_general(a, b, (((1,), (0,)), ((), ())), preferred_element_type=F32)


def rope(value, cos, front, back):
    return value * cos + pltpu.roll(value, 80, 1) * front + pltpu.roll(value, 48, 1) * back


def forward_kernel(
    dims,
    x, cot, cos, front, back, widen, widen_att, gain_cols, wq_s, gu_s, dn_s, wo_s,
    o_n1, o_qkv, o_lse, o_gh, o_att, o_block, o_ghid, o_wq, o_sgu, o_rgu, o_sdn,
    hid,
    nbuf, cbuf, qkv, wq, wqp, wo, gu, dn, act, ggu, att_out, att_in, gh_in, stg, sgu_t,
    wo_f, wq_b, gu_b, dn_b, wo_b,
    sc_stage, sc_in, sc_out, sc_inn,
    zw_a, zw_b, zw_c, zw_d, zo_a, zo_b, zo_c, zo_d, zd_a, zd_b, zd_c, zd_d,
    zg_a, zg_b, zg_c, zg_d, z_ss, z_sr, local, loads,
    n1_a, n1_b, n1_c, n1_d, ct_a, ct_b, ct_c, ct_d, n2_a, n2_b, n2_c, n2_d, wo_ga, wo_gb, wo_gc, wo_gd,
    rs_a, rs_b, rs_c, rs_d, ds_a, ds_b, ds_c, ds_d, at_s, at_r, gh_s, gh_r, near_s, near_r, free,
):
    n, sib, planes = dims
    at = Place(n, sib, planes)
    length, width = x.shape
    seq_len = n * length
    raw = len(wq_s.shape) == 2
    _, rows, head_cols = wq_b.shape
    owners = planes * sib
    chunks = GROUP * HEAD_DIM // rows
    units = dn_b.shape[0]
    local_units = planes * units
    parts = 2 if units % 128 == 0 else 1
    wide = local_units // parts
    part_cols = wo_b.shape[1]
    heads_per = rows // HEAD_DIM
    half_len = length // 2
    tau = at.s * sib + at.c
    scale = HEAD_DIM ** (-0.5)
    log2e = 1.4426950408889634
    sent = []

    def token_part(ref):
        return lambda c, s, h: ref.at[c, s, pl.ds(h * half_len, half_len)]

    def owner_rows(f):
        return pl.ds(pl.multiple_of(f * rows, rows), rows)

    if raw:
        gu_f = (o_ghid, hid)

        def cut(ref, k, lo, size, dst):
            return pltpu.make_async_copy(
                ref.at[:, pl.ds(pl.multiple_of(lo, 128), size)], dst, loads.at[k]
            )

        def wq_f(c):
            return gu_f[c].at[pl.ds(0, rows), pl.ds(2 * local_units, head_cols)]

        in_wq = [
            cut(wq_s, 3 + 2 * owners + c, (at.s * sib + c) * head_cols, head_cols, wq_f(c))
            for c in range(sib)
        ]
        in_wo = cut(wo_s, 1, at.s * part_cols, part_cols, wo_f)
        half_units = units // 2

        def dn_f(h):
            return gu_f[h].at[pl.ds(rows, half_units)]

        in_dn = [
            pltpu.make_async_copy(
                dn_s.at[pl.ds(pl.multiple_of(at.s * units + h * half_units, half_units), half_units)],
                dn_f(h), loads.at[2 * h],
            )
            for h in range(2)
        ]
        in_gu = []

        def gu_lane(p, g):
            return p * units // wide * 2 * wide + g * wide + p * units % wide

        for c in range(sib):
            for p in range(planes):
                for g in range(2):
                    lo = (g * owners + p * sib + c) * (n * units) + at.s * units
                    k = (c * planes + p) * 2 + g
                    in_gu.append(
                        cut(gu_s, 3 + k, lo, units,
                            gu_f[c].at[pl.ds(0, rows), pl.ds(gu_lane(p, g), units)])
                    )
        for copy in (*in_wq, in_wo, *in_dn, *in_gu):
            copy.start()
        wq_x, gu_x, dn_x, wo_x = wq_b, gu_b, dn_b, wo_b
    else:
        wq_x, gu_x, dn_x, wo_x = wq_s, gu_s, dn_s, wo_s

    move_wq = Move(at, lambda c: wq_x.at[c], lambda f: wq.at[owner_rows(f)], (zw_a, zw_b, zw_c, zw_d))
    move_wo = Move(
        at, lambda c: wo_x, lambda f: wo.at[lax.rem(f, sib), at.s, lax.div(f, sib)],
        (zo_a, zo_b, zo_c, zo_d), False,
    )
    move_dn = Move(
        at, lambda c: dn_x,
        lambda f: dn.at[pl.ds(pl.multiple_of(lax.div(f, sib) * units, units), units)],
        (zd_a, zd_b, zd_c, zd_d), False,
    )

    def gu_move(k):
        return Move(
            at, lambda c: gu_x.at[k, c], lambda f: gu.at[k, owner_rows(f)],
            (zg_a.at[k], zg_b.at[k], zg_c.at[k], zg_d.at[k]),
        )

    move_gu = [gu_move(k) for k in range(parts)]

    x_f = x[...].astype(F32)
    inv_one = lax.rsqrt(jnp.mean(x_f * x_f, axis=-1, keepdims=True) + NORM_EPS)
    nbuf[at.c, at.s] = (x_f * inv_one).astype(BF)
    cbuf[at.c, at.s] = cot[...]
    n_one = Gather(at, token_part(nbuf), (n1_a, n1_b, n1_c, n1_d))
    at.barrier()
    n_one.start()
    if raw:
        g_one = gain_cols[:, 0:1]
        for c in range(sib):
            in_wq[c].wait()
            wq_b[c] = (wq_f(c)[...] * g_one).astype(BF)
        in_wo.wait()
        wo_b[...] = wo_f[...].astype(BF)
    move_wq.start()
    if raw:
        for h in range(2):
            in_dn[h].wait()
            dn_b[h * half_units : (h + 1) * half_units] = dn_f(h)[...].astype(BF)
        for copy in in_gu:
            copy.wait()
        g_two = gain_cols[:, 1:2]
        for c in range(sib):
            for k in range(parts):
                lanes = slice(k * 2 * wide, (k + 1) * 2 * wide)
                gu_b[k, c] = (gu_f[c][0:rows, lanes] * g_two).astype(BF)
    n_stages = list(n_one.stages())
    n_one.hop_first(1)
    move_wq.pass_on()
    move_wo.start()
    n_one.hop_second(1)
    for h, _ in n_stages[2:-1]:
        n_one.hop(h)
    move_wq.wait()
    move_gu[0].start_far()

    @pl.loop(0, width // 256)
    def _(t):
        here = pl.ds(pl.multiple_of(t * 256, 256), 256)
        wqp[here] = nn(wq[here], widen[...]).astype(BF)

    save_wq = pltpu.make_async_copy(wqp, o_wq, local.at[2])
    save_wq.start()

    def project(c, s):
        y = nn(nbuf[c, s], wqp[...]).astype(BF)
        here = pl.ds(pl.multiple_of(s * length, length), length)
        cs, fr, bk = cos[here], front[here], back[here]
        for k in range(3):
            lanes = slice(128 * k, 128 * k + 128)
            qkv[c, here, lanes] = rope(y[:, lanes].astype(F32), cs, fr, bk).astype(BF)
        qkv[c, here, 384:512] = y[:, 384:512]

    for h, offsets in n_stages:
        if h == n // 2:
            n_one.hop(h)
        for j in offsets:
            n_one.sib_wait(j)
            s_j = at.seq_at(j)

            @pl.loop(0, sib)
            def _(c):
                project(c, s_j)

    cot_gather = Gather(at, token_part(cbuf), (ct_a, ct_b, ct_c, ct_d))
    save_n1 = pltpu.make_async_copy(nbuf, o_n1, local.at[3])
    save_n1.start()
    save_qkv = pltpu.make_async_copy(qkv, o_qkv, local.at[4])
    save_qkv.start()

    tri = lax.broadcasted_iota(jnp.int32, (length, length), 0) >= lax.broadcasted_iota(
        jnp.int32, (length, length), 1
    )

    def spot(k, b, i):
        return (k * sib + b) * n + i

    def attend(i):
        @pl.loop(0, sib)
        def _(b):
            past = i * length
            here = slice(past, past + length)
            outs = []
            for h in range(GROUP):
                q = qkv[b, here, 128 * h : 128 * h + 128]
                d = jnp.where(tri, nt(q, qkv[b, here, 256:384]) * (scale * log2e), -1e30)
                m = jnp.max(d, axis=1, keepdims=True)
                if i:
                    e = nt(q, qkv[b, 0:past, 256:384]) * (scale * log2e)
                    m = jnp.maximum(m, jnp.max(e, axis=1, keepdims=True))
                d = jnp.exp2(d - m)
                total = jnp.sum(d, axis=1, keepdims=True)
                o = nn(d.astype(BF), qkv[b, here, 384:512])
                if i:
                    e = jnp.exp2(e - m)
                    total = total + jnp.sum(e, axis=1, keepdims=True)
                    o = o + nn(e.astype(BF), qkv[b, 0:past, 384:512])
                outs.append((o / total).astype(BF))
                lse = jnp.broadcast_to(m + jnp.log2(total), (length, 128))
                o_lse[b, h, i] = lse.T[0:8]
            for k in range(chunks):
                pair = jnp.concatenate(outs[k * heads_per : (k + 1) * heads_per], axis=1)
                att_out[spot(k, b, i)] = nt(pair, widen_att[...]).astype(BF)

    def send_attended(i):
        for k in range(chunks):
            for b in range(sib):
                mine = jnp.logical_and(at.s == i, at.c == b)

                @pl.when(mine)
                def _():
                    att_in[tau * chunks + k] = att_out[spot(k, b, i)]

                @pl.when(jnp.logical_not(mine))
                def _():
                    rdma(att_out.at[spot(k, b, i)], att_in.at[tau * chunks + k], at_s.at[k, b, i],
                         at_r.at[tau * chunks + k], at.dev(i, b)).start()

    wo_gather = Gather(
        at, lambda c, s, h: wo.at[c, s, pl.ds(h * (planes // 2), planes // 2)],
        (wo_ga, wo_gb, wo_gc, wo_gd),
    )
    attend(n - 1)
    save_n1.wait()
    n_one.drain()
    send_attended(n - 1)
    move_wo.pass_on()
    move_wo.wait()
    wo_gather.start()
    move_gu[0].start_near()
    for move in move_gu[1:]:
        move.start_far()
    for i in range(n - 2, -1, -1):
        attend(i)
        send_attended(i)
    wo_hops = list(wo_gather.stages())
    for h, _ in wo_hops[1:-1]:
        wo_gather.hop(h)
    cot_gather.start()
    wo_gather.hop(n // 2)
    for _, offsets in wo_hops:
        for j in offsets:
            wo_gather.sib_wait(j)
    wo_gather.drain()
    save_qkv.wait()
    save_wq.wait()

    group = n * sib
    for j in range(1, group):
        t = lax.rem(tau + j, group)
        for k in range(chunks):
            ref = att_in.at[t * chunks + k]
            rdma(ref, ref, at_s.at[0, 0, 0], at_r.at[t * chunks + k], at.dev(at.s, at.c)).wait_recv()
    for k in range(chunks):
        for i in range(n):
            for b in range(sib):
                @pl.when(jnp.logical_not(jnp.logical_and(at.s == i, at.c == b)))
                def _():
                    rdma(att_out.at[spot(k, b, i)], att_out.at[spot(k, b, i)], at_s.at[k, b, i],
                         at_r.at[0], at.dev(at.s, at.c)).wait_send()
    save_att = pltpu.make_async_copy(att_in, o_att, local.at[3])
    save_att.start()

    x_f = x[...].astype(F32)
    for s in range(n):
        cols = slice(s * part_cols, (s + 1) * part_cols)
        acc = x_f[:, cols]
        for p in range(planes):
            for c in range(sib):
                acc = acc + nn(att_in[p * sib + c], wo[c, s, p])
        hid[:, cols] = acc
    hidden = hid[...]
    inv_mid = lax.rsqrt(jnp.mean(hidden * hidden, axis=-1, keepdims=True) + NORM_EPS)
    nbuf[at.c, at.s] = (hidden * inv_mid).astype(BF)
    n_two = Gather(at, token_part(nbuf), (n2_a, n2_b, n2_c, n2_d))
    n_two.start()

    stages = list(n_two.stages())
    move_dn.start_far()
    for move in move_gu[1:]:
        move.start_near()
    move_gu[0].pass_on()
    for h, _ in stages[1:-1]:
        cot_gather.hop(h)
    for move in move_gu[1:]:
        move.pass_on()
    move_dn.start_near()
    for h, _ in stages[1:-1]:
        n_two.hop(h)
    move_dn.pass_on()

    def gate_pass(k, c, s):
        y = nn(nbuf[c, s], gu[k])
        gate, up = y[:, :wide], y[:, wide:]
        act[c, s, :, k * wide : (k + 1) * wide] = (gate / (1.0 + jnp.exp(-gate)) * up).astype(BF)
        ggu[c, s, :, k * 2 * wide : (k + 1) * 2 * wide] = y.astype(BF)

    def grad_pass(c, s):
        for k in range(parts):
            lo = k * 2 * wide
            gate = ggu[c, s, :, lo : lo + wide].astype(F32)
            up = ggu[c, s, :, lo + wide : lo + 2 * wide].astype(F32)
            grad_act = nt(cbuf[c, s], dn[k * wide : (k + 1) * wide])
            sig = 1.0 / (1.0 + jnp.exp(-gate))
            ggu[c, s, :, lo : lo + wide] = (
                grad_act * up * sig * (1.0 + gate * (1.0 - sig))
            ).astype(BF)
            ggu[c, s, :, lo + wide : lo + 2 * wide] = (grad_act * (gate * sig)).astype(BF)

    def each_block(offsets, body):
        for j in offsets:
            s_j = at.seq_at(j)

            @pl.loop(0, sib)
            def _(c):
                body(c, s_j)

    def rows_wait(offsets):
        for j in offsets:
            n_two.sib_wait(j)
            cot_gather.sib_wait(j)

    early = [j for _, offsets in stages[:-1] for j in offsets]
    late = stages[-1][1]
    rows_wait(early)
    for k in range(parts):
        move_gu[k].wait()
        each_block(early, lambda c, s: gate_pass(k, c, s))
    move_dn.wait()
    each_block(early, grad_pass)
    n_two.hop(n // 2)
    cot_gather.hop(n // 2)
    rows_wait(late)
    for k in range(parts):
        each_block(late, lambda c, s: gate_pass(k, c, s))
    each_block(late, grad_pass)

    scatter = Scatter(
        at, Scatter.views(sc_stage, sc_in, sc_out, sc_inn), (rs_a, rs_b, rs_c, rs_d), length, width
    )
    tile = 512

    def column_tiles():
        return [slice(t * tile, (t + 1) * tile) for t in range(width // tile)]

    def mid_part(c, s, cols):
        acc = nt(ggu[c, s, :, 0 : 2 * wide], gu[0, cols, :])
        for k in range(1, parts):
            acc = acc + nt(ggu[c, s, :, k * 2 * wide : (k + 1) * 2 * wide], gu[k, cols, :])
        return acc

    def to_stage(c, s, ref):
        for cols in column_tiles():
            ref[:, cols] = mid_part(c, s, cols).astype(BF)

    def to_ring(c, s, store):
        for cols in column_tiles():
            store(cols, mid_part(c, s, cols))

    tokens = sib * seq_len
    down_copies = []

    def grad_down():
        cot_all = cbuf[...].reshape(tokens, width)
        down_rows = local_units // 2
        for t in range(2):
            rows_here = slice(t * down_rows, (t + 1) * down_rows)
            lhs = act[:, :, :, rows_here].reshape(tokens, down_rows)
            stg[rows_here] = tn(lhs, cot_all).astype(BF)
        own = pltpu.make_async_copy(
            stg.at[pl.ds(pl.multiple_of(at.p * units, units), units)], o_sdn.at[at.p], local.at[6]
        )
        own.start()
        down_copies.append(own)
        for dp in range(1, planes):
            to = lax.rem(at.p + dp, planes)
            copy = rdma(stg.at[pl.ds(pl.multiple_of(to * units, units), units)], o_sdn.at[at.p],
                        z_ss.at[dp], z_sr.at[dp], (at.s, at.col(dp, 0)))
            copy.start()
            sent.append(copy)

    gu_tile = sgu_t.shape[1]
    gu_steps = width // gu_tile
    near = planes == 4

    def gu_copy(m, slot):
        return pltpu.make_async_copy(
            sgu_t.at[slot], o_sgu.at[pl.ds(m * gu_tile, gu_tile)], local.at[7 + slot]
        )

    def near_send(m, dc):
        to = m * sib + lax.rem(at.c + dc, sib)
        return rdma(o_sgu.at[owner_rows(to)], o_rgu.at[at.f], near_s.at[m, dc],
                    near_r.at[at.p, dc], (at.s, to))

    def if_near(m, body):
        pl.when(jnp.logical_or(at.p == m - 1, at.p == m + 1))(body)

    def leave(m):
        gu_copy(m, m % 2).wait()
        if near:
            for dc in range(sib):
                if_near(m, lambda: near_send(m, dc).start())

    def grad_gu():
        for m in range(gu_steps):
            slot = m % 2
            lhs = nbuf[:, :, :, m * gu_tile : (m + 1) * gu_tile].reshape(tokens, gu_tile)
            sgu_t[slot] = tn(lhs, ggu[...].reshape(tokens, 2 * local_units)).astype(BF)
            gu_copy(m, slot).start()
            if m:
                leave(m - 1)
        leave(gu_steps - 1)

    def finish(cols, value):
        o_ghid[:, cols] = value

    def flat(ref, base):
        return lambda w, k: ref.at[base, w * (n // 2) + k]

    down = Scatter(
        at, (lambda k: cbuf.at[0, k], lambda k: nbuf.at[0, k], flat(cbuf, sib - 1), flat(nbuf, sib - 1)),
        (ds_a, ds_b, ds_c, ds_d), length, width,
    )

    def down_stage(c, s, ref):
        for cols in column_tiles():
            ref[:, cols] = nn(act[c, s], dn[:, cols]).astype(BF)

    def down_ring(c, s, store):
        for cols in column_tiles():
            store(cols, nn(act[c, s], dn[:, cols]))

    def down_finish(cols, value):
        o_block[:, cols] = (hid[:, cols] + value).astype(BF)

    credits = Credits(at, free)
    last = len(scatter.offsets()) - 1
    scatter.open(to_stage, to_ring, finish)
    grad_down()
    for k in range(1, last):
        scatter.step(k, to_ring, finish)
    grad_gu()
    cot_gather.drain()
    n_two.drain()
    credits.give()
    credits.take()
    down.open(down_stage, down_ring, down_finish)
    scatter.step(last, to_ring, finish)
    e_mid = o_ghid[...]
    hidden = hid[...]
    inv_mid = lax.rsqrt(jnp.mean(hidden * hidden, axis=-1, keepdims=True) + NORM_EPS)
    norm_mid = hidden * inv_mid
    o_ghid[...] = cot[...].astype(F32) + inv_mid * (
        e_mid - norm_mid * jnp.mean(e_mid * norm_mid, axis=-1, keepdims=True)
    )
    branch = o_ghid[...].astype(BF)
    for f in range(owners):
        p, c = f // sib, f % sib
        acc = nt(branch[:, :part_cols], wo[c, 0, p])
        for s in range(1, n):
            acc = acc + nt(branch[:, s * part_cols : (s + 1) * part_cols], wo[c, s, p])
        att_out[f] = acc.astype(BF)
        t, k = f // chunks, f % chunks
        mine = tau == t

        @pl.when(mine)
        def _():
            gh_in[k, at.c, at.s] = att_out[f]

        @pl.when(jnp.logical_not(mine))
        def _():
            rdma(att_out.at[f], gh_in.at[k, at.c, at.s], gh_s.at[f], gh_r.at[k, tau],
                 at.dev(t // sib, t % sib)).start()

    for k in range(1, last):
        down.step(k, down_ring, down_finish)
    for j in range(1, group):
        t = lax.rem(tau + j, group)
        for k in range(chunks):
            ref = gh_in.at[k, lax.rem(t, sib), lax.div(t, sib)]
            rdma(ref, ref, gh_s.at[0], gh_r.at[k, t], at.dev(at.s, at.c)).wait_recv()
    save_gh = pltpu.make_async_copy(gh_in, o_gh, local.at[0])
    save_gh.start()
    for f in range(owners):
        @pl.when(jnp.logical_not(tau == f // chunks))
        def _():
            rdma(att_out.at[f], att_out.at[f], gh_s.at[f], gh_r.at[0, 0],
                 at.dev(at.s, at.c)).wait_send()

    down.step(last, down_ring, down_finish)

    for dp in range(1, planes):
        ref = o_sdn.at[lax.rem(at.p - dp + planes, planes)]
        rdma(ref, ref, z_ss.at[dp], z_sr.at[dp], (at.s, at.f)).wait_recv()
    for copy in down_copies:
        copy.wait()
    if near:
        for q in range(planes):
            for dc in range(sib):
                def arrived():
                    ref = o_rgu.at[q * sib + lax.rem(at.c - dc + sib, sib)]
                    rdma(ref, ref, near_s.at[q, dc], near_r.at[q, dc], (at.s, at.f)).wait_recv()
                    near_send(q, dc).wait_send()

                if_near(q, arrived)
    scatter.drain()
    down.drain()
    for move in (move_wq, move_wo, move_dn, *move_gu):
        move.drain()
    for copy in sent:
        copy.wait_send()
    save_att.wait()
    save_gh.wait()


def forward_call(dims, sizes, x, cot, tables, widen, widen_att, gain_cols, wq_s, gu_s, dn_s, wo_s):
    n, sib, planes = dims
    rows, units = sizes
    length, width = x.shape
    part_cols = width // n
    head_cols = (GROUP + 2) * HEAD_DIM
    owners = planes * sib
    chunks = GROUP * HEAD_DIM // rows
    ffl = planes * units
    parts = 2 if units % 128 == 0 else 1
    seq_len = n * length
    vm, hb = pl.BlockSpec(memory_space=pltpu.VMEM), pl.BlockSpec(memory_space=pl.ANY)
    blocks = (sib, n, length, width)
    sds = jax.ShapeDtypeStruct
    outs = [
        (sds(blocks, BF), hb),
        (sds((sib, seq_len, 512), BF), hb),
        (sds((sib, GROUP, n, 8, length), F32), vm),
        (sds((chunks, sib, n, length, rows), BF), hb),
        (sds((owners, length, rows), BF), hb),
        (sds((length, width), BF), vm),
        (sds((length, width), F32), vm),
        (sds((width, 512), BF), hb),
        (sds((width, 2 * ffl), BF), hb),
        (sds((owners, rows, 2 * ffl), BF), hb),
        (sds((planes, units, width), BF), hb),
    ]
    dma = pltpu.SemaphoreType.DMA
    scratch = [
        pltpu.VMEM((length, width), F32),
        pltpu.VMEM(blocks, BF), pltpu.VMEM(blocks, BF), pltpu.VMEM((sib, seq_len, 512), BF),
        pltpu.VMEM((width, head_cols), BF), pltpu.VMEM((width, 512), BF),
        pltpu.VMEM((sib, n, planes, rows, part_cols), BF),
        pltpu.VMEM((parts, width, 2 * ffl // parts), BF), pltpu.VMEM((ffl, width), BF),
        pltpu.VMEM((sib, n, length, ffl), BF), pltpu.VMEM((sib, n, length, 2 * ffl), BF),
        pltpu.VMEM((owners, length, rows), BF), pltpu.VMEM((owners, length, rows), BF),
        pltpu.VMEM((chunks, sib, n, length, rows), BF),
        pltpu.VMEM((ffl, width), BF), pltpu.VMEM((2, 384, 2 * ffl), BF),

        pltpu.VMEM((rows, part_cols), F32),
        pltpu.VMEM((sib, rows, head_cols), BF),
        pltpu.VMEM((parts, sib, rows, 2 * ffl // parts), BF),
        pltpu.VMEM((units, width), BF), pltpu.VMEM((rows, part_cols), BF),
        *Scatter.scratch(n, (length, width)),
        *Move.sems(planes, sib), *Move.sems(planes, sib), *Move.sems(planes, sib),
        dma((parts, planes, sib)), dma((parts, planes, sib)), dma((parts, sib)), dma((parts, 1)),
        dma((planes,)), dma((planes,)), dma((9,)), dma((3 + 2 * owners + sib,)),
        *Gather.scratch(n), *Gather.scratch(n), *Gather.scratch(n), *Gather.scratch(n),
        *Scatter.sems(n), *Scatter.sems(n),
        dma((chunks, sib, n)), dma((owners,)), dma((owners,)), dma((chunks, n * sib)),
        dma((planes, sib)), dma((planes, sib)), pltpu.SemaphoreType.REGULAR,
    ]
    return pl.pallas_call(
        functools.partial(forward_kernel, dims),
        out_shape=[o[0] for o in outs],
        out_specs=[o[1] for o in outs],
        in_specs=[vm] * 8 + [hb] * 4,
        scratch_shapes=scratch,
        compiler_params=pltpu.CompilerParams(
            collective_id=0, has_side_effects=True, vmem_limit_bytes=VMEM_LIMIT
        ),
    )(x, cot, *tables, widen, widen_att, gain_cols, wq_s, gu_s, dn_s, wo_s)


def backward_kernel(
    dims,
    x, cos, front, back, widen, widen_att, lse,
    n1, qkv_h, gh_h, att_h, ghid, wqp_h, sgu, rgu_h, sdn_h,
    o_input, o_gq, o_ggu, o_gdn, o_gout,
    qkv, gh, att, wqp, sdn, gq, gk, gv, n1_t, sq, so, branch,
    r_gu, r_qkv, r_out, g_gu, g_qkv, g_dn, g_out,
    sc_stage, sc_in, sc_out, sc_inn, free,
    via, via_s, via_r, loads, near_l, saves_gu, saves_qkv, saves_row, z_gs, z_gr, z_qs, z_qr, z_os, z_or,
    e_a, e_b, e_c, e_d, s_a, s_b, s_c, s_d,
    a_dn_s, a_dn_r, a_gu_s, a_gu_r, a_qk_s, a_qk_r, a_ou_s, a_ou_r,
):
    n, sib, planes = dims
    at = Place(n, sib, planes)
    length, width = x.shape
    owners = planes * sib
    chunks, _, _, _, rows = gh.shape
    heads_per = rows // HEAD_DIM
    part_cols = r_out.shape[2]
    scale = HEAD_DIM ** (-0.5)
    log2e = 1.4426950408889634
    tokens = sib * n * length
    sent = []
    near = planes == 4
    units = g_dn.shape[1]
    aligned = len(o_ggu.shape) == 2

    def load(src, dst, k):
        copy = pltpu.make_async_copy(src, dst, loads.at[k])
        copy.start()
        return copy

    def owner_rows(f):
        return pl.ds(pl.multiple_of(f * rows, rows), rows)

    def z_source(dp, dc):
        return (
            lax.rem(at.p - dp + planes, planes) * sib + lax.rem(at.c - dc + sib, sib)
        )

    def z_scatter(src, dst, ssem, rsem, k):
        own = load(src.at[owner_rows(at.f)], dst.at[at.f], k)
        for dp in range(planes):
            for dc in range(sib):
                if dp or dc:
                    to = at.col(dp, dc)
                    copy = rdma(src.at[owner_rows(to)], dst.at[at.f],
                                ssem.at[dp, dc], rsem.at[dp, dc], (at.s, to))
                    copy.start()
                    sent.append(copy)
        return own

    def z_collect(dst, ssem, rsem, own):
        own.wait()
        for dp in range(planes):
            for dc in range(sib):
                if dp or dc:
                    ref = dst.at[z_source(dp, dc)]
                    rdma(ref, ref, ssem.at[dp, dc], rsem.at[dp, dc], (at.s, at.f)).wait_recv()

    def plane_total(dst, c):
        acc = dst[c].astype(F32)
        for p in range(1, planes):
            acc = acc + dst[p * sib + c].astype(F32)
        return acc.astype(BF)

    def gu_pairs():
        for dp in [2, 0] if near else range(planes):
            for dc in range(sib):
                if dp or dc:
                    yield dp, dc

    def at_ends(body):
        pl.when(jnp.logical_or(at.p == 0, at.p == planes - 1))(body)

    def at_middle(body):
        pl.when(jnp.logical_and(at.p != 0, at.p != planes - 1))(body)

    def gu_from(dp, dc):
        return at_ends if near and dp == 2 else lambda body: body()

    def gu_copy(src, dp, dc):
        to = at.col(dp, dc)
        return rdma(src, r_gu.at[at.f], z_gs.at[dp, dc], z_gr.at[dp, dc], (at.s, to))

    def gu_send(dp, dc):
        return gu_copy(sgu.at[owner_rows(at.col(dp, dc))], dp, dc)

    def plane_rows(p):
        return pl.ds(pl.multiple_of(p * (sib * rows), sib * rows), sib * rows)

    def toward_middle():
        far_plane = planes - 1 - at.p
        beside = at.p + 1 - 2 * lax.div(at.p, planes - 1)
        return rdma(sgu.at[plane_rows(far_plane)], via.at[0], via_s.at[0], via_r.at[0],
                    (at.s, beside * sib + at.c))

    def sum_load():
        return pltpu.make_async_copy(
            sgu.at[plane_rows(lax.rem(at.p + 2, planes))], via.at[1], loads.at[12]
        )

    def gu_send_sum(dc):
        c = lax.rem(at.c + dc, sib)
        return gu_copy(via.at[1, pl.ds(pl.multiple_of(c * rows, rows), rows)], 2, dc)

    def sum_on():
        def body():
            ref = via.at[0]
            rdma(ref, ref, via_s.at[0], via_r.at[0], (at.s, at.f)).wait_recv()
            sum_load().wait()
            via[1] = (via[0].astype(F32) + via[1].astype(F32)).astype(BF)
            for dc in range(sib):
                gu_send_sum(dc).start()

        at_middle(body)

    def gu_near(q, dc):
        f = q * sib + dc
        return pltpu.make_async_copy(rgu_h.at[f], r_gu.at[f], near_l.at[q, dc])

    def if_near(q, body):
        pl.when(jnp.logical_or(at.p == q - 1, at.p == q + 1))(body)

    def gu_wait(dp, dc):
        ref = r_gu.at[z_source(dp, dc)]
        rdma(ref, ref, z_gs.at[dp, dc], z_gr.at[dp, dc], (at.s, at.f)).wait_recv()

    at.barrier()
    in_qkv, in_gh = load(qkv_h, qkv, 0), load(gh_h, gh, 1)
    in_sdn, in_att, in_wqp = load(sdn_h, sdn, 4), load(att_h, att, 6), load(wqp_h, wqp, 7)
    gu_own = load(sgu.at[owner_rows(at.f)], r_gu.at[at.f], 5)
    if near:
        at_ends(lambda: toward_middle().start())
        at_middle(lambda: sum_load().start())
    for dp, dc in gu_pairs():
        gu_from(dp, dc)(lambda: gu_send(dp, dc).start())
    if near:
        for q in range(planes):
            for dc in range(sib):
                if_near(q, lambda: gu_near(q, dc).start())
    n1_cols = n1_t.shape[4]
    n1_steps = width // n1_cols

    def n1_load(m):
        return pltpu.make_async_copy(
            n1.at[:, :, :, pl.ds(m * n1_cols, n1_cols)], n1_t.at[m % 2], loads.at[8 + m % 2]
        )

    n1_load(0).start()
    n1_load(1).start()

    def row_half(ref):
        size = ref.shape[-2] // 2
        if len(ref.shape) == 4:
            return lambda c, s, h: ref.at[s, :, pl.ds(h * size, size)]
        return lambda c, s, h: ref.at[s, pl.ds(h * size, size)]

    in_sdn.wait()
    acc = sdn[0].astype(F32)
    for p in range(1, planes):
        acc = acc + sdn[p].astype(F32)
    g_dn[at.s] = acc.astype(BF)
    ag_dn = Gather(at, row_half(g_dn), (a_dn_s, a_dn_r))
    ag_dn.start()

    tri = lax.broadcasted_iota(jnp.int32, (length, length), 0) <= lax.broadcasted_iota(
        jnp.int32, (length, length), 1
    )

    def attend_back(b):
        gk[...] = jnp.zeros_like(gk)
        gv[...] = jnp.zeros_like(gv)
        for i in range(n):
            past = i * length
            here = slice(past, past + length)
            for h in range(GROUP):
                k, slot = h // heads_per, h % heads_per
                q = qkv[b, here, 128 * h : 128 * h + 128]
                do = nn(gh[k, b, i], widen_att[:, 128 * slot : 128 * slot + 128]).astype(BF)
                row = lse[b, h, i, 0:1]
                parts = [(here, True)] + ([(slice(0, past), False)] if i else [])
                probs, grads = [], []
                delta = 0.0
                for part, diagonal in parts:
                    sc = nt(qkv[b, part, 256:384], q) * (scale * log2e)
                    if diagonal:
                        sc = jnp.where(tri, sc, -1e30)
                    pr = jnp.exp2(sc - row)
                    dp = nt(qkv[b, part, 384:512], do)
                    delta = delta + jnp.sum(pr * dp, axis=0, keepdims=True)
                    probs.append(pr)
                    grads.append(dp)
                dq = jnp.zeros((length, 128), F32)
                for (part, _), pr, dp in zip(parts, probs, grads):
                    ds = (pr * (dp - delta) * scale).astype(BF)
                    gv[part] += nn(pr.astype(BF), do)
                    gk[part] += nn(ds, q)
                    dq = dq + tn(ds, qkv[b, part, 256:384])
                gq[b, here, 128 * h : 128 * h + 128] = rope(
                    dq, cos[here], -front[here], -back[here]
                ).astype(BF)
        for i in range(n):
            here = slice(i * length, (i + 1) * length)
            gq[b, here, 256:384] = rope(gk[here], cos[here], -front[here], -back[here]).astype(BF)
            gq[b, here, 384:512] = gv[here].astype(BF)

    tile = 512

    def tiles():
        return [slice(t * tile, (t + 1) * tile) for t in range(width // tile)]

    last = len(Scatter(at, (None,) * 4, (None,) * 4, rows, width).offsets()) - 1
    hops = n // 2

    s_out = Scatter(
        at, Scatter.views(sc_stage, sc_in, sc_out, sc_inn), (s_a, s_b, s_c, s_d),
        rows, planes * part_cols,
    )
    for s in range(n):
        branch[s] = ghid[:, s * part_cols : (s + 1) * part_cols].astype(BF)

    def out_pieces(c, s):
        low = branch[s]
        for p in range(planes):
            yield slice(p * part_cols, (p + 1) * part_cols), tn(att[p * sib + c], low)

    def out_stage(c, s, ref):
        for cols, value in out_pieces(c, s):
            ref[:, cols] = value.astype(BF)

    def out_ring(c, s, store):
        for cols, value in out_pieces(c, s):
            store(cols, value)

    def out_finish(cols, value):
        so[cols.start // part_cols] = value.astype(BF)

    in_att.wait()
    s_out.open(out_stage, out_ring, out_finish)
    in_qkv.wait()
    in_gh.wait()
    attend_back(0)
    ag_dn.hop(1)
    for k in range(1, last):
        s_out.step(k, out_ring, out_finish)
    if sib > 1:
        attend_back(1)
    for h in range(2, hops + 1):
        ag_dn.hop(h)
    s_out.step(last, out_ring, out_finish)
    s_out.drain()
    credits = Credits(at, free)
    credits.give()

    for m in range(n1_steps):
        n1_load(m).wait()
        part = tn(n1_t[m % 2].reshape(tokens, n1_cols), gq[...].reshape(tokens, 512)).astype(BF)
        sq[m * n1_cols : (m + 1) * n1_cols] = nt(part, widen[...]).astype(BF)
        if m + 2 < n1_steps:
            n1_load(m + 2).start()

    if near:
        sum_on()

    in_wqp.wait()
    e_in = Scatter(
        at, Scatter.views(sc_stage, sc_in, sc_out, sc_inn), (e_a, e_b, e_c, e_d), length, width
    )

    def gq_block(c, s):
        return gq[c, pl.ds(pl.multiple_of(s * length, length), length)]

    def e_stage(c, s, ref):
        for cols in tiles():
            ref[:, cols] = nt(gq_block(c, s), wqp[cols, :]).astype(BF)

    def e_ring(c, s, store):
        for cols in tiles():
            store(cols, nt(gq_block(c, s), wqp[cols, :]))

    def e_finish(cols, value):
        o_input[:, cols] = value

    credits.take()
    e_in.open(e_stage, e_ring, e_finish)
    for k in range(1, last):
        e_in.step(k, e_ring, e_finish)

    gu_own.wait()
    if near:
        for q in range(planes):
            for dc in range(sib):
                if_near(q, lambda: gu_near(q, dc).wait())
    for dp, dc in gu_pairs():
        gu_wait(dp, dc)
    if near:
        for c in range(sib):
            @pl.when(at.p == 0)
            def _():
                r_gu[(planes - 1) * sib + c] = jnp.zeros(r_gu.shape[1:], BF)

            @pl.when(at.p == planes - 1)
            def _():
                r_gu[c] = jnp.zeros(r_gu.shape[1:], BF)
    qkv_own = z_scatter(sq, r_qkv, z_qs, z_qr, 10)
    out_own = load(so.at[at.p], r_out.at[at.p], 11)
    for dp in range(1, planes):
        to = lax.rem(at.p + dp, planes)
        copy = rdma(so.at[to], r_out.at[at.p], z_os.at[dp], z_or.at[dp], (at.s, at.col(dp, 0)))
        copy.start()
        sent.append(copy)
    for c in range(sib):
        g_gu[at.s, c] = plane_total(r_gu, c)
    ag_gu = Gather(at, row_half(g_gu), (a_gu_s, a_gu_r))
    ag_gu.start()

    wide = planes * units // 2

    def gu_lane(p, g):
        return p * units // wide * 2 * wide + g * wide + p * units % wide

    def save_gu(j):
        s = at.seq_at(j)
        slot = j % n
        if not aligned:
            return [pltpu.make_async_copy(g_gu.at[s], o_ggu.at[s], saves_gu.at[slot, 0])]
        copies = []
        for c in range(sib):
            for p in range(planes):
                for g in range(2):
                    lo = (g * owners + p * sib + c) * (n * units) + s * units
                    copies.append(pltpu.make_async_copy(
                        g_gu.at[s, c, :, pl.ds(gu_lane(p, g), units)],
                        o_ggu.at[:, pl.ds(pl.multiple_of(lo, 128), units)],
                        saves_gu.at[slot, (c * planes + p) * 2 + g],
                    ))
        return copies

    def save_qkv(j):
        s = at.seq_at(j)
        slot = j % n
        if not aligned:
            return [pltpu.make_async_copy(g_qkv.at[s], o_gq.at[s], saves_qkv.at[slot, 0])]
        cols = g_qkv.shape[3]
        return [
            pltpu.make_async_copy(
                g_qkv.at[s, c], o_gq.at[:, pl.ds(pl.multiple_of((s * sib + c) * cols, 128), cols)],
                saves_qkv.at[slot, c],
            )
            for c in range(sib)
        ]

    def save_out(j):
        s = at.seq_at(j)
        slot = j % n
        if not aligned:
            return [pltpu.make_async_copy(g_out.at[s], o_gout.at[s], saves_row.at[0, slot])]
        place = o_gout.at[:, pl.ds(pl.multiple_of(s * part_cols, 128), part_cols)]
        return [pltpu.make_async_copy(g_out.at[s], place, saves_row.at[0, slot])]

    def save_down(j):
        s = at.seq_at(j)
        place = o_gdn.at[pl.ds(pl.multiple_of(s * units, units), units)]
        return [pltpu.make_async_copy(g_dn.at[s], place, saves_row.at[1, j % n])]

    saves = []

    def save(copies):
        for copy in copies:
            copy.start()
        saves.extend(copies)

    ring = [0] + [j for h in range(1, hops) for j in (-h, h)] + [hops]
    for j in ring:
        save(save_down(j))
    e_in.step(last, e_ring, e_finish)
    x_f = x[...].astype(F32)
    inv_one = lax.rsqrt(jnp.mean(x_f * x_f, axis=-1, keepdims=True) + NORM_EPS)
    norm_one = x_f * inv_one
    e_val = o_input[...]
    o_input[...] = ghid[...] + inv_one * (
        e_val - norm_one * jnp.mean(e_val * norm_one, axis=-1, keepdims=True)
    )
    out_own.wait()
    for dp in range(1, planes):
        ref = r_out.at[lax.rem(at.p - dp + planes, planes)]
        rdma(ref, ref, z_os.at[dp], z_or.at[dp], (at.s, at.f)).wait_recv()
    acc = r_out[0].astype(F32)
    for p in range(1, planes):
        acc = acc + r_out[p].astype(F32)
    g_out[at.s] = acc.astype(BF)
    ag_out = Gather(at, row_half(g_out), (a_ou_s, a_ou_r))
    ag_out.start()
    save(save_out(0))
    save(save_gu(0))
    z_collect(r_qkv, z_qs, z_qr, qkv_own)
    for c in range(sib):
        g_qkv[at.s, c] = plane_total(r_qkv, c)
    ag_qkv = Gather(at, row_half(g_qkv), (a_qk_s, a_qk_r))
    ag_qkv.start()
    save(save_qkv(0))
    for h in range(1, hops + 1):
        for ag, put in ((ag_gu, save_gu), (ag_out, save_out), (ag_qkv, save_qkv)):
            ag.hop(h)
            for j in (-h, h) if h < hops else (h,):
                save(put(j))
    e_in.drain()
    for ag in (ag_dn, ag_gu, ag_qkv, ag_out):
        ag.drain()
    for dp, dc in gu_pairs():
        gu_from(dp, dc)(lambda: gu_send(dp, dc).wait_send())
    if near:
        at_ends(lambda: toward_middle().wait_send())
        for dc in range(sib):
            at_middle(lambda: gu_send_sum(dc).wait_send())
    for copy in sent:
        copy.wait_send()
    for copy in saves:
        copy.wait()


def backward_call(dims, aligned, x, tables, widen, widen_att, lse, n1, qkv, gh, att, ghid, wqp, sgu, rgu, sdn):
    n, sib, planes = dims
    length, width = x.shape
    rows = gh.shape[4]
    owners = planes * sib
    units = sdn.shape[1]
    part_cols = width // n
    seq_len = n * length
    head_cols = (GROUP + 2) * HEAD_DIM
    vm, hb = pl.BlockSpec(memory_space=pltpu.VMEM), pl.BlockSpec(memory_space=pl.ANY)
    sds = jax.ShapeDtypeStruct
    g_shapes = [
        (n, sib, rows, head_cols), (n, sib, rows, sgu.shape[1]), (n, units, width),
        (n, rows, part_cols),
    ]
    o_shapes = g_shapes
    if aligned:
        o_shapes = [
            (rows, n * sib * head_cols), (rows, n * sib * sgu.shape[1]), None, (rows, width)
        ]
    o_shapes = [*o_shapes[:2], (n * units, width), o_shapes[3]]
    outs = [(sds((length, width), F32), vm)] + [(sds(shape, BF), hb) for shape in o_shapes]
    dma = pltpu.SemaphoreType.DMA
    scratch = [
        pltpu.VMEM(qkv.shape, BF), pltpu.VMEM(gh.shape, BF), pltpu.VMEM(att.shape, BF),
        pltpu.VMEM(wqp.shape, BF), pltpu.VMEM(sdn.shape, BF), pltpu.VMEM(qkv.shape, BF),
        pltpu.VMEM((seq_len, 128), F32), pltpu.VMEM((seq_len, 128), F32),
        pltpu.VMEM((2, *n1.shape[:3], 384), BF), pltpu.VMEM((width, head_cols), BF),
        pltpu.VMEM((planes, rows, part_cols), BF), pltpu.VMEM((n, length, part_cols), BF),
        pltpu.VMEM((owners, rows, sgu.shape[1]), BF), pltpu.VMEM((owners, rows, head_cols), BF),
        pltpu.VMEM((planes, rows, part_cols), BF),
        pltpu.VMEM(g_shapes[1], BF), pltpu.VMEM(g_shapes[0], BF), pltpu.VMEM(g_shapes[2], BF),
        pltpu.VMEM(g_shapes[3], BF),
        *Scatter.scratch(n, (length, max(width, planes * part_cols))),
        pltpu.SemaphoreType.REGULAR,
        pltpu.VMEM((2, sib * rows, sgu.shape[1]), BF), dma((1,)), dma((1,)),
        dma((13,)), dma((planes, sib)), dma((n, 2 * owners)), dma((n, sib)), dma((2, n)),
        dma((planes, sib)), dma((planes, sib)), dma((planes, sib)),
        dma((planes, sib)), dma((planes,)), dma((planes,)),
        *Scatter.sems(n), *Scatter.sems(n),
        *Gather.scratch(n, False), *Gather.scratch(n, False), *Gather.scratch(n, False),
        *Gather.scratch(n, False),
    ]
    return pl.pallas_call(
        functools.partial(backward_kernel, dims),
        out_shape=[o[0] for o in outs],
        out_specs=[o[1] for o in outs],
        in_specs=[vm] * 7 + [hb] * 4 + [vm] + [hb] * 4,
        scratch_shapes=scratch,
        compiler_params=pltpu.CompilerParams(
            collective_id=1, has_side_effects=True, vmem_limit_bytes=BACK_LIMIT
        ),
    )(x, *tables, widen, widen_att, lse, n1, qkv, gh, att, ghid, wqp, sgu, rgu, sdn)


def adamw(weight, first, second, grad, rate, decay):
    first_new = BETA_ONE * first + (1.0 - BETA_ONE) * grad
    second_new = BETA_TWO * second + (1.0 - BETA_TWO) * grad * grad
    first_hat = first_new / (1.0 - BETA_ONE**ADAM_STEP)
    second_hat = second_new / (1.0 - BETA_TWO**ADAM_STEP)
    weight_new = weight - rate * (first_hat / (jnp.sqrt(second_hat) + ADAM_EPS) + decay * weight)
    return (weight_new, first_new, second_new)


def to_bf16(value):
    return lax.reduce_precision(value, exponent_bits=8, mantissa_bits=7)


def rope_arrays(seq_len):
    half = HEAD_DIM // 2
    frequencies = (ROPE_BASE ** (-(2.0 * np.arange(half)) / HEAD_DIM)).astype(np.float32)
    angles = np.arange(seq_len, dtype=np.float32)[:, None] * frequencies[None, :]
    cos, sin = np.cos(angles), np.sin(angles)
    pad = np.zeros((seq_len, 128 - HEAD_DIM), np.float32)
    none = np.zeros_like(sin)
    return tuple(
        np.concatenate(columns, axis=1).astype(np.float32)
        for columns in ([cos, cos, pad], [-sin, none, pad], [none, sin, pad])
    )


def widening(heads):
    row = np.arange(heads * HEAD_DIM)[:, None]
    col = np.arange(heads * 128)[None, :]
    return (col == row // HEAD_DIM * 128 + row % HEAD_DIM).astype(ml_dtypes.bfloat16)


def make(n_seq, n_fsdp):
    sib = KV_HEADS // n_seq
    planes = n_fsdp // sib

    def on_device(
        inputs, cotangent, qkv_weight, out_weight, gate_up_weight, down_weight, norm_gains,
        qkv_first, qkv_second, out_first, out_second, gate_up_first, gate_up_second,
        down_first, down_second, gain_first, gain_second,
    ):
        s_idx = lax.axis_index("seq")
        _, length, width = inputs.shape
        seq_len = length * n_seq
        rows = qkv_weight.shape[0]
        head_cols = (GROUP + 2) * HEAD_DIM
        ff_rows = down_weight.shape[0]
        units = ff_rows // n_seq
        hidden_units = ff_rows * n_fsdp
        part_cols = width // n_seq
        aligned = units % 128 == 0 and part_cols % 128 == 0 and sib == 2
        aligned = aligned and rows + units // 2 <= length
        gains = to_bf16(norm_gains)
        gain_cols = gains.T

        if aligned:
            pieces = (qkv_weight, gate_up_weight, down_weight, out_weight)
        else:
            wq_s = lax.dynamic_slice_in_dim(
                qkv_weight, s_idx * sib * head_cols, sib * head_cols, 1
            )
            wq_s = (wq_s * gains[0][:, None]).astype(BF).reshape(rows, sib, head_cols)
            gu_s = gate_up_weight.reshape(rows, 2, planes, sib, n_seq, units)
            gu_s = lax.dynamic_index_in_dim(gu_s, s_idx, 4, keepdims=False)
            gu_s = (gu_s * gains[1][:, None, None, None, None]).astype(BF)
            gu_s = gu_s.transpose(3, 0, 1, 2, 4).reshape(1, sib, rows, 2 * planes * units)
            dn_s = lax.dynamic_slice_in_dim(down_weight, s_idx * units, units, 0).astype(BF)
            wo_s = lax.dynamic_slice_in_dim(out_weight, s_idx * part_cols, part_cols, 1).astype(BF)
            pieces = (wq_s.transpose(1, 0, 2), gu_s, dn_s, wo_s)
        tables = tuple(jnp.asarray(table) for table in rope_arrays(seq_len))
        widen = jnp.asarray(widening(GROUP + 2))
        widen_att = jnp.asarray(widening(rows // HEAD_DIM))

        n_one, qkv, lse, gh, att, block_out, grad_hidden, w_qkv, s_gu, r_gu, s_down = forward_call(
            (n_seq, sib, planes), (rows, units), inputs[0], cotangent[0], tables, widen, widen_att,
            gain_cols, *pieces,
        )
        input_grad, g_qkv, g_gu, g_down, g_out = backward_call(
            (n_seq, sib, planes), aligned, inputs[0], tables, widen, widen_att, lse, n_one, qkv, gh,
            att, grad_hidden, w_qkv, s_gu, r_gu, s_down,
        )
        block_out, input_grad = block_out[None], input_grad[None]
        if not aligned:
            g_qkv = g_qkv.transpose(2, 0, 1, 3).reshape(rows, n_seq * sib * head_cols)
            g_gu = g_gu.reshape(n_seq, sib, rows, 2, planes, units).transpose(2, 3, 4, 1, 0, 5)
            g_gu = g_gu.reshape(rows, 2 * hidden_units)
            g_out = g_out.transpose(1, 0, 2).reshape(rows, width)
        g_qkv, g_gu, g_down, g_out = (g.astype(F32) for g in (g_qkv, g_gu, g_down, g_out))
        gain_grad = jnp.stack(
            [
                jnp.sum(g_qkv * to_bf16(qkv_weight), axis=1),
                jnp.sum(g_gu * to_bf16(gate_up_weight), axis=1),
            ]
        )
        g_qkv = g_qkv * gains[0][:, None]
        g_gu = g_gu * gains[1][:, None]
        qkv_new = adamw(qkv_weight, qkv_first, qkv_second, g_qkv, RATE_QKV, WEIGHT_DECAY)
        out_new = adamw(out_weight, out_first, out_second, g_out, RATE_OUT, WEIGHT_DECAY)
        gu_new = adamw(
            gate_up_weight, gate_up_first, gate_up_second, g_gu, RATE_GATE_UP, WEIGHT_DECAY
        )
        down_new = adamw(
            down_weight, down_first, down_second, g_down, RATE_DOWN, WEIGHT_DECAY
        )
        gains_new = adamw(norm_gains, gain_first, gain_second, gain_grad, RATE_GAINS, 0.0)
        return (block_out, input_grad, *qkv_new, *out_new, *gu_new, *down_new, *gains_new)

    return on_device


def solution(mesh):
    tokens = P("fsdp", "seq", None)
    weight = P("fsdp", None)
    gain = P(None, "fsdp")
    in_specs = (tokens, tokens, weight, weight, weight, weight, gain) + (weight,) * 8 + (gain,) * 2
    out_specs = (tokens, tokens) + (weight,) * 12 + (gain,) * 3
    return jax.shard_map(
        make(mesh.shape["seq"], mesh.shape["fsdp"]),
        mesh=mesh, in_specs=in_specs, out_specs=out_specs, check_vma=False,
    )
```

profile of v0, /device:TPU:8, one launch (start us, length us, event | category | flops | bytes accessed | tf_op | source)
XLA Modules:
  0.0 392.5 jit_solution(16483621303637889278)
XLA Ops:
  0.7 0.8 copy.40
  1.5 0.7 fusion.22
  2.1 213.7 %shard_map.341 = (bf16[2,4,256,1536]{3,2,1,0:T(8,128)(2,1)}, bf16[2,1024,512]{2,1,0:T(8,128)(2,1)}, f32[2,2,4,8,256]{4,3,2,1,0:T(8,128)}, bf16[1,2,4,256,192]{4,...) custom-call(bf16[256,1536]{1,0:T(8,128)(2,1)} %bitcast.8, ...), custom_call_target="tpu_custom_call" | custom-call | tf_op jit(solution)/shard_map/pallas_call | solution.py:1003
  215.8 0.0 copy-done
  215.8 0.0 copy-done.1
  215.9 0.0 copy-done.2
  215.9 0.0 copy-done.8
  215.9 0.0 copy-start.3
  215.9 1.0 copy-done.3
  216.9 1.4 copy-done.4
  218.3 1.0 copy-done.5
  219.3 1.2 copy-done.6
  220.6 1.2 copy-done.7
  221.8 0.9 copy-done.9
  222.7 140.4 %shard_map.342 = (f32[256,1536]{1,0:T(8,128)S(1)}, bf16[192,3072]{1,0:T(8,128)(2,1)S(1)}, bf16[192,8192]{1,0:T(8,128)(2,1)}, bf16[512,1536]{1,0:T(8,128)(2,1)S(1)}, bf16[192,1536]{1,0:T(8,128)(2,1)S(1)}) custom-call(bf16[256,1536]{1,0:T(8,128)(2,1)S(1)} %bitcast.9, f32[1024,128]{1,0:T(8,128)S(1)} %copy-done.1, f32[1024,128]{1,0:T(8,128)S(1)} %copy-done.2, ...), custom_call_target="tpu_custom_call" | custom-call | tf_op jit(solution)/shard_map/pallas_call | solution.py:1480
  363.1 0.2 slice_reduce_fusion
  363.3 0.0 slice-start
  363.3 0.0 copy-start.12
  363.3 0.0 copy-start.16
  363.3 0.0 copy-start.17
  363.4 0.0 slice-start.1
  363.4 4.8 %multiply_subtract_fusion.2 = (f32[192,3072]{1,0:T(8,128)}, f32[192,3072]{1,0:T(8,128)}, f32[192,3072]{1,0:T(8,128)}, f32[192]{0:T(256)S(1)}) fusion(f32[192,3072]{1,0:T(8,128)S(1)} %copy-done.11, f32[192]{0:T(256)S(1)} %get-tuple-element.50, bf16[192,3072]{1,0:T(8,128)(2,1)S(1)} %get-tuple-element.45, f32[192,3072]{1,0:T(8,128)S(1)} %copy-done.14, ...), kind=kLoop, calls=%fused_computation.20 | loop fusion | flops 11796288 | bytes 15336960 | tf_op jit(solution)/shard_map/sub | solution.py:1497
  368.2 2.4 multiply_subtract_fusion.3
  370.6 0.0 copy-start.13
  370.7 12.7 %multiply_subtract_fusion = (f32[192,8192]{1,0:T(8,128)}, f32[192,8192]{1,0:T(8,128)}, f32[192,8192]{1,0:T(8,128)}, f32[192]{0:T(256)S(1)}) fusion(f32[192,8192]{1,0:T(8,128)S(1)} %bitcast.12, f32[192]{0:T(256)S(1)} %get-tuple-element.49, bf16[192,8192]{1,0:T(8,128)(2,1)} %get-tuple-element.47, f32[192,8192]{1,0:T(8,128)} %param.33, f32[192,8192]{1,0:T(8,128)} %param.34), kind=kLoop, calls=%fused_computation.7 | loop fusion | flops 31457088 | bytes 40896000 | tf_op jit(solution)/shard_map/sub | solution.py:1497
  383.4 0.0 copy-start.19
  383.4 0.0 copy-start.20
  383.4 0.0 copy-start.21
  383.4 6.0 %multiply_subtract_fusion.1 = (f32[512,1536]{1,0:T(8,128)}, f32[512,1536]{1,0:T(8,128)}, f32[512,1536]{1,0:T(8,128)}) fusion(f32[512,1536]{1,0:T(8,128)S(1)} %copy-done.10, bf16[512,1536]{1,0:T(8,128)(2,1)S(1)} %get-tuple-element.48, f32[512,1536]{1,0:T(8,128)S(1)} %copy-done.13, f32[512,1536]{1,0:T(8,128)} %param.36), kind=kLoop, calls=%fused_computation.13 | loop fusion | flops 12582912 | bytes 20447232 | tf_op jit(solution)/shard_map/sub | solution.py:1497
  389.4 0.6 multiply_subtract_fusion.4
  390.0 0.9 copy.43
  390.9 1.1 copy.44
  (29 shorter events, 0.1 us)
Async XLA Ops:
  2.1 213.7 %copy-start = (bf16[1,256,1536]{2,1,0:T(8,128)(2,1)S(1)}, bf16[1,256,1536]{2,1,0:T(8,128)(2,1)}, u32[]{:S(2)}) copy-start(bf16[1,256,1536]{2,1,0:T(8,128)(2,1)} %param.22) | copy-start | bytes 2359300
  2.1 213.7 %copy-start.1 = (f32[1024,128]{1,0:T(8,128)S(1)}, f32[1024,128]{1,0:T(8,128)}, u32[]{:S(2)}) copy-start(f32[1024,128]{1,0:T(8,128)} %constant.29.clone.cos) | copy-start | bytes 1572868
  2.1 213.7 %copy-start.2 = (f32[1024,128]{1,0:T(8,128)S(1)}, f32[1024,128]{1,0:T(8,128)}, u32[]{:S(2)}) copy-start(f32[1024,128]{1,0:T(8,128)} %constant.30.clone.front) | copy-start | bytes 1572868
  2.1 213.8 %copy-start.8 = (bf16[192,256]{1,0:T(8,128)(2,1)S(1)}, bf16[192,256]{1,0:T(8,128)(2,1)}, u32[]{:S(2)}) copy-start(bf16[192,256]{1,0:T(8,128)(2,1)} %constant.33.clone.widen_att) | copy-start | bytes 294916
  215.9 1.0 copy-start.3
  216.9 1.4 copy-start.4
  218.3 1.0 copy-start.5
  219.3 1.2 copy-start.6
  220.6 1.2 copy-start.7
  221.8 0.9 copy-start.9
  222.7 140.6 %copy-start.11 = (f32[192,3072]{1,0:T(8,128)S(1)}, f32[192,3072]{1,0:T(8,128)}, u32[]{:S(2)}) copy-start(f32[192,3072]{1,0:T(8,128)} %wq_s.1) | copy-start | bytes 7077892
  222.7 140.6 %copy-start.14 = (f32[192,3072]{1,0:T(8,128)S(1)}, f32[192,3072]{1,0:T(8,128)}, u32[]{:S(2)}) copy-start(f32[192,3072]{1,0:T(8,128)} %param.29) | copy-start | bytes 7077892
  222.7 140.6 %copy-start.15 = (f32[192,3072]{1,0:T(8,128)S(1)}, f32[192,3072]{1,0:T(8,128)}, u32[]{:S(2)}) copy-start(f32[192,3072]{1,0:T(8,128)} %param.30) | copy-start | bytes 7077892
  363.3 7.4 %slice-start = ((s8[6291456]{0:T(1024)(128)(4,1)}), s8[4194304]{0:T(1024)(128)(4,1)S(1)}, s32[]{:S(2)}) async-start(s8[6291456]{0:T(1024)(128)(4,1)} %bitcast.11), calls=%async_computation | async-start | bytes 8388608
  363.3 4.9 %copy-start.12 = (f32[192,1536]{1,0:T(8,128)S(1)}, f32[192,1536]{1,0:T(8,128)}, u32[]{:S(2)}) copy-start(f32[192,1536]{1,0:T(8,128)} %wo_s.1) | copy-start | bytes 3538948
  363.3 4.9 %copy-start.16 = (f32[192,1536]{1,0:T(8,128)S(1)}, f32[192,1536]{1,0:T(8,128)}, u32[]{:S(2)}) copy-start(f32[192,1536]{1,0:T(8,128)} %param.31) | copy-start | bytes 3538948
  363.3 4.9 %copy-start.17 = (f32[192,1536]{1,0:T(8,128)S(1)}, f32[192,1536]{1,0:T(8,128)}, u32[]{:S(2)}) copy-start(f32[192,1536]{1,0:T(8,128)} %param.32) | copy-start | bytes 3538948
  363.4 7.3 %slice-start.1 = ((s8[6291456]{0:T(1024)(128)(4,1)}), s8[2097152]{0:T(1024)(128)(4,1)S(1)}, s32[]{:S(2)}) async-start(s8[6291456]{0:T(1024)(128)(4,1)} %bitcast.11), calls=%async_computation.1 | async-start | bytes 4194304
  370.6 12.7 %copy-start.10 = (f32[512,1536]{1,0:T(8,128)S(1)}, f32[512,1536]{1,0:T(8,128)}, u32[]{:S(2)}) copy-start(f32[512,1536]{1,0:T(8,128)} %dn_s.1) | copy-start | bytes 9437188
  370.6 12.7 %copy-start.13 = (f32[512,1536]{1,0:T(8,128)S(1)}, f32[512,1536]{1,0:T(8,128)}, u32[]{:S(2)}) copy-start(f32[512,1536]{1,0:T(8,128)} %param.35) | copy-start | bytes 9437188
  383.4 6.1 %copy-start.19 = (f32[2,192]{1,0:T(2,128)S(1)}, f32[2,192]{1,0:T(2,128)}, u32[]{:S(2)}) copy-start(f32[2,192]{1,0:T(2,128)} %param.28) | copy-start | bytes 4612
  383.4 6.1 %copy-start.20 = (f32[2,192]{1,0:T(2,128)S(1)}, f32[2,192]{1,0:T(2,128)}, u32[]{:S(2)}) copy-start(f32[2,192]{1,0:T(2,128)} %param.37) | copy-start | bytes 4612
  383.4 6.1 %copy-start.21 = (f32[2,192]{1,0:T(2,128)S(1)}, f32[2,192]{1,0:T(2,128)}, u32[]{:S(2)}) copy-start(f32[2,192]{1,0:T(2,128)} %param.38) | copy-start | bytes 4612
  383.4 6.7 %copy-start.18 = (bf16[256,1536]{1,0:T(8,128)(2,1)S(1)}, bf16[256,1536]{1,0:T(8,128)(2,1)}, u32[]{:S(2)}) copy-start(bf16[256,1536]{1,0:T(8,128)(2,1)} %get-tuple-element.33) | copy-start | bytes 2359300
where the time goes:
time: 398 us; the launch traced here: 393 us
  Pallas kernels  354 us (89%)
  other arithmetic  27.2 us (7%)
  local copies, waits for them, and re-layouts  9.91 us (2%)
    pallas_call x1, Pallas kernels, forward_call(): pl.pallas_call(functools.partial(forward_kernel, dims), out_shape=[o[0] f...  214 us
    pallas_call x1, Pallas kernels, backward_call(): pl.pallas_call(functools.partial(backward_kernel, dims), out_shape=[o[0]...  140 us
    sub x5, other arithmetic, adamw(): weight - rate * (first_hat / (jnp.sqrt(second_hat) + ADAM_EPS) + decay *...  26.6 us
    unnamed x51, local copies, waits for them, and re-layouts  9.7 us

commit v1 on v0

--- a/solution.py
+++ b/solution.py
@@ -1444,6 +1444,7 @@
     seq_len = n * length
     head_cols = (GROUP + 2) * HEAD_DIM
     vm, hb = pl.BlockSpec(memory_space=pltpu.VMEM), pl.BlockSpec(memory_space=pl.ANY)
+    far = pl.BlockSpec(memory_space=pltpu.HBM)
     sds = jax.ShapeDtypeStruct
     g_shapes = [
         (n, sib, rows, head_cols), (n, sib, rows, sgu.shape[1]), (n, units, width),
@@ -1481,7 +1482,7 @@
         functools.partial(backward_kernel, dims),
         out_shape=[o[0] for o in outs],
         out_specs=[o[1] for o in outs],
-        in_specs=[vm] * 7 + [hb] * 4 + [vm] + [hb] * 4,
+        in_specs=[vm] * 7 + [far] * 4 + [vm] + [far] * 4,
         scratch_shapes=scratch,
         compiler_params=pltpu.CompilerParams(
             collective_id=1, has_side_effects=True, vmem_limit_bytes=BACK_LIMIT

time: 398 us -> 398 us (level)
  no operation moved by 1% of the time
where the time goes in v1:
time: 398 us; the launch traced here: 393 us
  Pallas kernels  354 us (89%)
  other arithmetic  27.2 us (7%)
  local copies, waits for them, and re-layouts  9.91 us (2%)
    pallas_call x1, Pallas kernels, forward_call(): pl.pallas_call(functools.partial(forward_kernel, dims), out_shape=[o[0] f...  214 us
    pallas_call x1, Pallas kernels, backward_call(): pl.pallas_call(functools.partial(backward_kernel, dims), out_shape=[o[0]...  140 us
    sub x5, other arithmetic, adamw(): weight - rate * (first_hat / (jnp.sqrt(second_hat) + ADAM_EPS) + decay *...  26.6 us
    unnamed x51, local copies, waits for them, and re-layouts  9.7 us

profile of v1, /device:TPU:8, one launch (start us, length us, event | category | flops | bytes accessed | tf_op | source)
XLA Modules:
  0.0 392.5 jit_solution(16483621303637889278)
XLA Ops:
  0.7 0.8 copy.40
  1.5 0.7 fusion.22
  2.1 213.7 %shard_map.341 = (bf16[2,4,256,1536]{3,2,1,0:T(8,128)(2,1)}, bf16[2,1024,512]{2,1,0:T(8,128)(2,1)}, f32[2,2,4,8,256]{4,3,2,1,0:T(8,128)}, bf16[1,2,4,256,192]{4,...) custom-call(bf16[256,1536]{1,0:T(8,128)(2,1)} %bitcast.8, ...), custom_call_target="tpu_custom_call" | custom-call | tf_op jit(solution)/shard_map/pallas_call | solution.py:1003
  215.8 0.0 copy-done
  215.8 0.0 copy-done.1
  215.9 0.0 copy-done.2
  215.9 0.0 copy-done.8
  215.9 0.0 copy-start.3
  215.9 1.0 copy-done.3
  216.9 1.4 copy-done.4
  218.3 1.0 copy-done.5
  219.3 1.2 copy-done.6
  220.6 1.2 copy-done.7
  221.8 0.9 copy-done.9
  222.7 140.4 %shard_map.342 = (f32[256,1536]{1,0:T(8,128)S(1)}, bf16[192,3072]{1,0:T(8,128)(2,1)S(1)}, bf16[192,8192]{1,0:T(8,128)(2,1)}, bf16[512,1536]{1,0:T(8,128)(2,1)S(1)}, bf16[192,1536]{1,0:T(8,128)(2,1)S(1)}) custom-call(bf16[256,1536]{1,0:T(8,128)(2,1)S(1)} %bitcast.9, f32[1024,128]{1,0:T(8,128)S(1)} %copy-done.1, f32[1024,128]{1,0:T(8,128)S(1)} %copy-done.2, ...), custom_call_target="tpu_custom_call" | custom-call | tf_op jit(solution)/shard_map/pallas_call | solution.py:1481
  363.1 0.2 slice_reduce_fusion
  363.3 0.0 slice-start
  363.3 0.0 copy-start.12
  363.3 0.0 copy-start.16
  363.3 0.0 copy-start.17
  363.4 0.0 slice-start.1
  363.4 4.8 %multiply_subtract_fusion.2 = (f32[192,3072]{1,0:T(8,128)}, f32[192,3072]{1,0:T(8,128)}, f32[192,3072]{1,0:T(8,128)}, f32[192]{0:T(256)S(1)}) fusion(f32[192,3072]{1,0:T(8,128)S(1)} %copy-done.11, f32[192]{0:T(256)S(1)} %get-tuple-element.50, bf16[192,3072]{1,0:T(8,128)(2,1)S(1)} %get-tuple-element.45, f32[192,3072]{1,0:T(8,128)S(1)} %copy-done.14, ...), kind=kLoop, calls=%fused_computation.20 | loop fusion | flops 11796288 | bytes 15336960 | tf_op jit(solution)/shard_map/sub | solution.py:1498
  368.2 2.4 multiply_subtract_fusion.3
  370.6 0.0 copy-start.13
  370.7 12.7 %multiply_subtract_fusion = (f32[192,8192]{1,0:T(8,128)}, f32[192,8192]{1,0:T(8,128)}, f32[192,8192]{1,0:T(8,128)}, f32[192]{0:T(256)S(1)}) fusion(f32[192,8192]{1,0:T(8,128)S(1)} %bitcast.12, f32[192]{0:T(256)S(1)} %get-tuple-element.49, bf16[192,8192]{1,0:T(8,128)(2,1)} %get-tuple-element.47, f32[192,8192]{1,0:T(8,128)} %param.33, f32[192,8192]{1,0:T(8,128)} %param.34), kind=kLoop, calls=%fused_computation.7 | loop fusion | flops 31457088 | bytes 40896000 | tf_op jit(solution)/shard_map/sub | solution.py:1498
  383.4 0.0 copy-start.19
  383.4 0.0 copy-start.20
  383.4 0.0 copy-start.21
  383.4 6.0 %multiply_subtract_fusion.1 = (f32[512,1536]{1,0:T(8,128)}, f32[512,1536]{1,0:T(8,128)}, f32[512,1536]{1,0:T(8,128)}) fusion(f32[512,1536]{1,0:T(8,128)S(1)} %copy-done.10, bf16[512,1536]{1,0:T(8,128)(2,1)S(1)} %get-tuple-element.48, f32[512,1536]{1,0:T(8,128)S(1)} %copy-done.13, f32[512,1536]{1,0:T(8,128)} %param.36), kind=kLoop, calls=%fused_computation.13 | loop fusion | flops 12582912 | bytes 20447232 | tf_op jit(solution)/shard_map/sub | solution.py:1498
  389.4 0.6 multiply_subtract_fusion.4
  390.0 0.9 copy.43
  390.9 1.1 copy.44
  (29 shorter events, 0.1 us)
Async XLA Ops:
  2.1 213.7 %copy-start = (bf16[1,256,1536]{2,1,0:T(8,128)(2,1)S(1)}, bf16[1,256,1536]{2,1,0:T(8,128)(2,1)}, u32[]{:S(2)}) copy-start(bf16[1,256,1536]{2,1,0:T(8,128)(2,1)} %param.22) | copy-start | bytes 2359300
  2.1 213.7 %copy-start.1 = (f32[1024,128]{1,0:T(8,128)S(1)}, f32[1024,128]{1,0:T(8,128)}, u32[]{:S(2)}) copy-start(f32[1024,128]{1,0:T(8,128)} %constant.29.clone.cos) | copy-start | bytes 1572868
  2.1 213.7 %copy-start.2 = (f32[1024,128]{1,0:T(8,128)S(1)}, f32[1024,128]{1,0:T(8,128)}, u32[]{:S(2)}) copy-start(f32[1024,128]{1,0:T(8,128)} %constant.30.clone.front) | copy-start | bytes 1572868
  2.1 213.8 %copy-start.8 = (bf16[192,256]{1,0:T(8,128)(2,1)S(1)}, bf16[192,256]{1,0:T(8,128)(2,1)}, u32[]{:S(2)}) copy-start(bf16[192,256]{1,0:T(8,128)(2,1)} %constant.33.clone.widen_att) | copy-start | bytes 294916
  215.9 1.0 copy-start.3
  216.9 1.4 copy-start.4
  218.3 1.0 copy-start.5
  219.3 1.2 copy-start.6
  220.6 1.2 copy-start.7
  221.8 0.9 copy-start.9
  222.7 140.6 %copy-start.11 = (f32[192,3072]{1,0:T(8,128)S(1)}, f32[192,3072]{1,0:T(8,128)}, u32[]{:S(2)}) copy-start(f32[192,3072]{1,0:T(8,128)} %wq_s.1) | copy-start | bytes 7077892
  222.7 140.6 %copy-start.14 = (f32[192,3072]{1,0:T(8,128)S(1)}, f32[192,3072]{1,0:T(8,128)}, u32[]{:S(2)}) copy-start(f32[192,3072]{1,0:T(8,128)} %param.29) | copy-start | bytes 7077892
  222.7 140.6 %copy-start.15 = (f32[192,3072]{1,0:T(8,128)S(1)}, f32[192,3072]{1,0:T(8,128)}, u32[]{:S(2)}) copy-start(f32[192,3072]{1,0:T(8,128)} %param.30) | copy-start | bytes 7077892
  363.3 7.4 %slice-start = ((s8[6291456]{0:T(1024)(128)(4,1)}), s8[4194304]{0:T(1024)(128)(4,1)S(1)}, s32[]{:S(2)}) async-start(s8[6291456]{0:T(1024)(128)(4,1)} %bitcast.11), calls=%async_computation | async-start | bytes 8388608
  363.3 4.9 %copy-start.12 = (f32[192,1536]{1,0:T(8,128)S(1)}, f32[192,1536]{1,0:T(8,128)}, u32[]{:S(2)}) copy-start(f32[192,1536]{1,0:T(8,128)} %wo_s.1) | copy-start | bytes 3538948
  363.3 4.9 %copy-start.16 = (f32[192,1536]{1,0:T(8,128)S(1)}, f32[192,1536]{1,0:T(8,128)}, u32[]{:S(2)}) copy-start(f32[192,1536]{1,0:T(8,128)} %param.31) | copy-start | bytes 3538948
  363.3 4.9 %copy-start.17 = (f32[192,1536]{1,0:T(8,128)S(1)}, f32[192,1536]{1,0:T(8,128)}, u32[]{:S(2)}) copy-start(f32[192,1536]{1,0:T(8,128)} %param.32) | copy-start | bytes 3538948
  363.4 7.3 %slice-start.1 = ((s8[6291456]{0:T(1024)(128)(4,1)}), s8[2097152]{0:T(1024)(128)(4,1)S(1)}, s32[]{:S(2)}) async-start(s8[6291456]{0:T(1024)(128)(4,1)} %bitcast.11), calls=%async_computation.1 | async-start | bytes 4194304
  370.6 12.7 %copy-start.10 = (f32[512,1536]{1,0:T(8,128)S(1)}, f32[512,1536]{1,0:T(8,128)}, u32[]{:S(2)}) copy-start(f32[512,1536]{1,0:T(8,128)} %dn_s.1) | copy-start | bytes 9437188
  370.6 12.7 %copy-start.13 = (f32[512,1536]{1,0:T(8,128)S(1)}, f32[512,1536]{1,0:T(8,128)}, u32[]{:S(2)}) copy-start(f32[512,1536]{1,0:T(8,128)} %param.35) | copy-start | bytes 9437188
  383.4 6.1 %copy-start.19 = (f32[2,192]{1,0:T(2,128)S(1)}, f32[2,192]{1,0:T(2,128)}, u32[]{:S(2)}) copy-start(f32[2,192]{1,0:T(2,128)} %param.28) | copy-start | bytes 4612
  383.4 6.1 %copy-start.20 = (f32[2,192]{1,0:T(2,128)S(1)}, f32[2,192]{1,0:T(2,128)}, u32[]{:S(2)}) copy-start(f32[2,192]{1,0:T(2,128)} %param.37) | copy-start | bytes 4612
  383.4 6.1 %copy-start.21 = (f32[2,192]{1,0:T(2,128)S(1)}, f32[2,192]{1,0:T(2,128)}, u32[]{:S(2)}) copy-start(f32[2,192]{1,0:T(2,128)} %param.38) | copy-start | bytes 4612
  383.4 6.7 %copy-start.18 = (bf16[256,1536]{1,0:T(8,128)(2,1)S(1)}, bf16[256,1536]{1,0:T(8,128)(2,1)}, u32[]{:S(2)}) copy-start(bf16[256,1536]{1,0:T(8,128)(2,1)} %get-tuple-element.33) | copy-start | bytes 2359300
